TPU v7x, 32 devices: a whole 2x2x4 slice. The times are simulated.
32 devices in a mesh: seq: 8 (over y, x, core), dp: 4 (over z).
Axes of the slice: x: 2, y: 2, z: 4, core: 2. Of those that a mesh axis runs over, the one named last changes fastest.
Arguments:
- queries: bfloat16 [4, 4096, 2048], P('dp', 'seq'), may hold values from -5 to 5
- keys: bfloat16 [4, 4096, 2048], P('dp', 'seq'), may hold values from -5 to 5
- values: bfloat16 [4, 4096, 2048], P('dp', 'seq'), may hold values from -8 to 8
- out_weight: bfloat16 [2048, 4096], P(None, 'dp'), may hold values from -0.125 to 0.125
Outputs:
- projected: bfloat16 [4, 4096, 4096], P('dp', 'seq')
All inputs are finite; a program needn't handle non-finite values.
Results may differ from a plain program's by a relative error of at most 0.0061.
Values may be sent and summed in bfloat16 or wider, within the bound.
A program may use at most 192 MiB of HBM per device.

v0:
```python
import math

import jax
import jax.numpy as jnp
from jax import lax
from jax.sharding import PartitionSpec as P

CHANNEL_WIDTH = 128
SEGMENT_LENGTH = 256


def prefix(value, axis, join, neutral):
    count, mine = (lax.axis_size(axis), lax.axis_index(axis))
    pieces = jax.tree.map(lambda part: lax.all_gather(part, axis), value)
    subtotal = jax.tree.map(
        lambda part, zero: jnp.full_like(part, 0) + jnp.asarray(zero, part.dtype), value, neutral
    )

    def turn(position, subtotal):
        longer = join(subtotal, jax.tree.map(lambda part: part[position], pieces))
        return jax.tree.map(lambda new, old: jnp.where(position < mine, new, old), longer, subtotal)

    return lax.fori_loop(0, count - 1, turn, subtotal)


def shifted(block, axis, distance):
    devices = range(lax.axis_size(axis))
    route = [(i - distance, i) for i in devices if i - distance in devices]
    return lax.ppermute(block, axis, route)


def add_pair(earlier_pair, later_pair):
    return (earlier_pair[0] + later_pair[0], earlier_pair[1] + later_pair[1])


def per_device(queries, keys, values, out_weight):
    local_rows = queries.shape[1]
    feature_width = queries.shape[2]
    head_count = feature_width // CHANNEL_WIDTH
    local_blocks = local_rows // SEGMENT_LENGTH
    shard_count = lax.axis_size("seq")
    shard_index = lax.axis_index("seq")
    total_blocks = local_blocks * shard_count
    first_block = shard_index * local_blocks
    softmax_multiplier = 1.0 / math.sqrt(CHANNEL_WIDTH)
    faraway_offset_bias = math.log(SEGMENT_LENGTH)
    own_queries = queries[0]
    own_keys = keys[0]
    own_values = values[0]
    span_address_means = jnp.mean(
        own_keys.reshape(local_blocks, SEGMENT_LENGTH, feature_width), axis=1, dtype=jnp.float32
    ).astype(jnp.bfloat16)
    value_means = jnp.mean(
        own_values.reshape(local_blocks, SEGMENT_LENGTH, feature_width), axis=1, dtype=jnp.float32
    ).astype(jnp.bfloat16)
    empty_buffer = jnp.zeros((total_blocks, feature_width), jnp.bfloat16)
    slot_keys = lax.dynamic_update_slice_in_dim(empty_buffer, span_address_means, first_block, 0)
    slot_values = lax.dynamic_update_slice_in_dim(empty_buffer, value_means, first_block, 0)
    far_keys, far_values = prefix(
        (slot_keys, slot_values), "seq", add_pair, (empty_buffer, empty_buffer)
    )
    prev_keys, prev_values = shifted(
        (own_keys[local_rows - SEGMENT_LENGTH :], own_values[local_rows - SEGMENT_LENGTH :]),
        "seq",
        1,
    )
    near_keys = jnp.concatenate([prev_keys, own_keys], axis=0)
    near_values = jnp.concatenate([prev_values, own_values], axis=0)
    far_k = far_keys.reshape(total_blocks, head_count, CHANNEL_WIDTH)
    far_v = far_values.reshape(total_blocks, head_count, CHANNEL_WIDTH)
    far_index = jnp.arange(total_blocks, dtype=jnp.int32)
    group_rows = SEGMENT_LENGTH * math.gcd(local_blocks, max(1, 512 // SEGMENT_LENGTH))
    request_vectors = own_queries.reshape(group_rows, head_count, CHANNEL_WIDTH)
    address_vectors = near_keys.reshape(group_rows + SEGMENT_LENGTH, head_count, CHANNEL_WIDTH)
    value_rows = near_values.reshape(group_rows + SEGMENT_LENGTH, head_count, CHANNEL_WIDTH)
    query_local = 0 + jnp.arange(group_rows, dtype=jnp.int32)
    key_local = 0 - SEGMENT_LENGTH + jnp.arange(group_rows + SEGMENT_LENGTH, dtype=jnp.int32)
    query_blk = query_local // SEGMENT_LENGTH
    key_blk = key_local // SEGMENT_LENGTH
    within_block = (key_blk[None, :] == query_blk[:, None]) & (
        key_local[None, :] <= query_local[:, None]
    )
    preceding_segment = (key_blk[None, :] == query_blk[:, None] - 1) & (
        (key_blk[None, :] >= 0) | (shard_index > 0)
    )
    adjacent_similarity = (
        jnp.einsum(
            "qhd,khd->hqk", request_vectors, address_vectors, preferred_element_type=jnp.float32
        )
        * softmax_multiplier
    )
    adjacent_similarity = jnp.where(
        (within_block | preceding_segment)[None], adjacent_similarity, -jnp.inf
    )
    query_global = first_block + query_blk
    faraway_similarity = (
        jnp.einsum("qhd,jhd->hqj", request_vectors, far_k, preferred_element_type=jnp.float32)
        * softmax_multiplier
        + faraway_offset_bias
    )
    faraway_similarity = jnp.where(
        (far_index[None, :] < query_global[:, None] - 1)[None], faraway_similarity, -jnp.inf
    )
    row_max = jnp.maximum(
        jnp.max(adjacent_similarity, axis=-1), jnp.max(faraway_similarity, axis=-1)
    )[..., None]
    near_w = jnp.exp(adjacent_similarity - row_max)
    far_w = jnp.exp(faraway_similarity - row_max)
    row_total = jnp.sum(near_w, axis=-1, keepdims=True) + jnp.sum(far_w, axis=-1, keepdims=True)
    near_p = (near_w / row_total).astype(jnp.bfloat16)
    far_p = (far_w / row_total).astype(jnp.bfloat16)
    attended = jnp.einsum("hqk,khd->qhd", near_p, value_rows, preferred_element_type=jnp.float32)
    attended = attended + jnp.einsum(
        "hqj,jhd->qhd", far_p, far_v, preferred_element_type=jnp.float32
    )
    pieces = attended.astype(jnp.bfloat16).reshape(group_rows, feature_width)
    projected = jnp.dot(
        pieces,
        lax.all_gather(out_weight, "dp", axis=1, tiled=True),
        preferred_element_type=jnp.float32,
    ).astype(jnp.bfloat16)
    return projected[None]


def solution(mesh):
    return jax.shard_map(
        per_device,
        mesh=mesh,
        in_specs=(P("dp", "seq", None), P("dp", "seq", None), P("dp", "seq", None), P(None, "dp")),
        out_specs=P("dp", "seq", None),
        check_vma=False,
    )
```

profile of v0, /device:TPU:3, one launch (start us, length us, event | category | flops | bytes accessed | tf_op | source)
XLA Modules:
  0.0 318.5 jit_solution(8824105027232640933)
XLA Ops:
  6.5 0.0 copy-start
  6.5 0.0 all-gather.2.cloned.1.call-start
  6.5 0.7 all-gather.2.cloned.1.call-update
  7.3 3.9 %copy.25 = bf16[1,512,2048]{1,2,0:T(8,128)(2,1)} copy(bf16[1,512,2048]{2,1,0:T(8,128)(2,1)} %param.7) | data formatting | bytes 4194304 | tf_op args[1]
  11.2 2.3 slice_bitcast_fusion
  13.5 3.7 %collective-permute-start.1 = (bf16[256,2048]{0,1:T(8,128)(2,1)}, bf16[256,2048]{0,1:T(8,128)(2,1)}, u32[]{:S(2)}, u32[]{:S(2)}) collective-permute-start(bf16[256,2048]{0,1:T(8,128)(2,1)} %slice_bitcast_fusion), channel_id=1, source_target_pairs={{0,4},{4,8},{8,12},{12,16},{16,20},{20,24},{24,28},{1,5},{5,9},{9,... | collective-permute-start | bytes 3145736 | tf_op jit(solution)/shard_map/ppermute | solution.py:29
  17.2 0.0 copy-done
  17.2 1.1 slice_bitcast_fusion.1
  18.2 1.9 collective-permute-start
  20.2 2.6 copy.24
  22.7 3.8 %copy.37 = bf16[64,8,16,128]{3,2,1,0:T(8,128)(2,1)} copy(bf16[64,8,16,128]{3,1,2,0:T(8,128)(2,1)} %bitcast.70) | data formatting | bytes 4194304
  26.5 4.0 %copy.28 = bf16[512,16,128]{2,0,1:T(8,128)(2,1)} copy(bf16[512,16,128]{0,2,1:T(8,128)(2,1)} %bitcast.68) | data formatting | bytes 4194304 | tf_op jit(solution)/shard_map/concatenate | solution.py:67
  30.5 2.0 convert_reduce_fusion.1
  32.6 14.4 %all_gather.11 = bf16[8,16,2048]{2,1,0:T(8,128)(2,1)S(1)} all-gather(bf16[1,16,2048]{2,1,0:T(8,128)(2,1)S(1)} %fusion.39), channel_id=1, replica_groups=mesh['seq'=8,'dp'=4] {'seq'}, dimensions={0}, use_global_device_ids=true | all-gather | bytes 589824 | tf_op jit(solution)/shard_map/all_gather | solution.py:14
  47.0 0.4 convert_reduce_fusion
  47.4 9.2 %all_gather.12 = bf16[8,16,2048]{2,1,0:T(8,128)(2,1)S(1)} all-gather(bf16[1,16,2048]{2,1,0:T(8,128)(2,1)S(1)} %fusion.41), channel_id=1, replica_groups=mesh['seq'=8,'dp'=4] {'seq'}, dimensions={0}, use_global_device_ids=true | all-gather | bytes 589824 | tf_op jit(solution)/shard_map/all_gather | solution.py:14
  56.6 0.6 while.16
  56.6 0.1 add_select_fusion.5
  56.7 0.1 add_select_fusion.5
  56.8 0.1 add_select_fusion.5
  56.9 0.1 add_select_fusion.5
  56.9 0.1 add_select_fusion.5
  57.0 0.1 add_select_fusion.5
  57.1 0.1 add_select_fusion.5
  57.2 0.8 fusion.17
  58.1 2.5 fusion.52
  60.6 0.0 collective-permute-done.1
  60.6 1.6 copy.27
  62.2 13.5 %fusion.1 = (f32[16,512]{1,0:T(8,128)S(1)}, f32[16,768,512]{2,1,0:T(8,128)}) fusion(pred[512,768]{0,1:T(8,128)(4,1)S(1)} %fusion.17, bf16[512,16,128]{2,1,0:T(8,128)(2,1)} %bitcast.73, bf16[512,16,128]{2,0,1:T(8,128)(2,1)} %copy.28, bf16[256,16,128]{2,0,1:T(8,128)(2,1)S(1)} %copy.27), kind=kOutput, calls=%fused_computation.6 | convolution fusion | flops 1635770368 | bytes 30834688 | tf_op jit(solution)/shard_map/qhd,khd->hqk/dot_general | solution.py:87
  75.8 0.1 fusion.30
  75.9 11.2 %fusion = f32[16,512]{1,0:T(8,128)S(1)} fusion(f32[16,768,512]{2,1,0:T(8,128)} %get-tuple-element.153, f32[16,512]{1,0:T(8,128)S(1)} %max.7, pred[512,768]{0,1:T(8,128)(4,1)S(1)} %fusion.17), kind=kLoop, calls=%fused_computation.5 | loop fusion | flops 25157632 | bytes 25624576 | tf_op jit(solution)/shard_map/reduce_sum | solution.py:109
  87.2 0.0 collective-permute-done
  87.2 1.5 copy.23
  88.7 2.8 fusion.31
  91.4 14.7 %add_convert_fusion = bf16[16,128,512]{2,1,0:T(8,128)(2,1)} fusion(f32[16,128,512]{2,1,0:T(8,128)} %fusion.31, f32[16,768,512]{2,1,0:T(8,128)} %get-tuple-element.153, f32[16,512]{1,0:T(8,128)S(1)} %add.130, f32[16,512]{1,0:T(8,128)S(1)} %max.7, pred[512,768]{0,1:T(8,128)(4,1)S(1)} %fusion.17, bf16[512,16,128]{0,2,1:T(8,128)(2,1)} %bitcast.71, ...), kind=kOutput, calls=%fused_computation.12 | convolution fusion | flops 1650458624 | bytes 35061760 | tf_op jit(solution)/shard_map/hqk,khd->qhd/dot_general | solution.py:112
  106.2 191.0 %all-gather.2.cloned.1.call-done = bf16[2048,4096]{1,0:T(8,128)(2,1)} async-done(((bf16[2048,1024]{1,0:T(8,128)(2,1)}), bf16[2048,4096]{1,0:T(8,128)(2,1)}) %all-gather.2.cloned.1.call-update) | async-done | bytes 16777232 | tf_op jit(solution)/shard_map/all_gather | solution.py:119
  297.2 14.5 %fusion.3 = bf16[1,512,4096]{2,1,0:T(8,128)(2,1)} fusion(bf16[512,2048]{0,1:T(8,128)(2,1)} %bitcast.75, bf16[2048,4096]{1,0:T(8,128)(2,1)} %all-gather.2.cloned.1.call-done), kind=kOutput, calls=%fused_computation.9 | convolution fusion | flops 8592031744 | bytes 23068672 | tf_op jit(solution)/shard_map/dot_general | solution.py:117
  (13 shorter events, 0.1 us)
Async XLA Ops:
  6.5 10.6 %copy-start = (bf16[1,512,2048]{2,1,0:T(8,128)(2,1)S(1)}, bf16[1,512,2048]{2,1,0:T(8,128)(2,1)}, u32[]{:S(2)}) copy-start(bf16[1,512,2048]{2,1,0:T(8,128)(2,1)} %param.8) | copy-start | bytes 6291460
  6.5 290.6 %all-gather.2.cloned.1.call-start = ((), (), s32[]{:S(2)}) async-start(), calls=%async_computation | async-start | bytes 20971520 | tf_op jit(solution)/shard_map/all_gather | solution.py:119
  13.5 47.1 %collective-permute-start.1 = (bf16[256,2048]{0,1:T(8,128)(2,1)}, bf16[256,2048]{0,1:T(8,128)(2,1)}, u32[]{:S(2)}, u32[]{:S(2)}) collective-permute-start(bf16[256,2048]{0,1:T(8,128)(2,1)} %slice_bitcast_fusion), channel_id=1, source_target_pairs={{0,4},{4,8},{8,12},{12,16},{16,20},{20,24},{24,28},{1,5},{5,9},{9,... | collective-permute-start | bytes 3145736 | tf_op jit(solution)/shard_map/ppermute | solution.py:29
  18.2 69.0 %collective-permute-start = (bf16[256,2048]{1,0:T(8,128)(2,1)}, bf16[256,2048]{1,0:T(8,128)(2,1)}, u32[]{:S(2)}, u32[]{:S(2)}) collective-permute-start(bf16[256,2048]{1,0:T(8,128)(2,1)} %slice_bitcast_fusion.1), channel_id=1, source_target_pairs={{0,4},{4,8},{8,12},{12,16},{16,20},{20,24},{24,28},{1,5},{5,9},{9,... | collective-permute-start | bytes 3145736 | tf_op jit(solution)/shard_map/ppermute | solution.py:29
Sparse Core Ops, SparseCore 0:
  8.9 288.2 all-gather.1
where the time goes:
time: 320 us; the launch traced here: 318 us
  waiting for transfers between devices  192 us (60%)
  matrix products  48 us (15%)
  blocking collectives  23.6 us (7%)
  local copies, waits for them, and re-layouts  20.7 us (6%)
  other arithmetic  15.1 us (5%)
  between operations  13.6 us (4%)
  starting transfers between devices  5.58 us (2%)
    all_gather x1, waiting for transfers between devices, per_device(): lax.all_gather(out_weight, 'dp', axis=1, tiled=True)  191 us
    all_gather x2, blocking collectives, prefix(): pieces = jax.tree.map(lambda part: lax.all_gather(part, axis), value)  23.6 us
    dot_general x1, matrix products, per_device(): jnp.einsum('hqk,khd->qhd', near_p, value_rows, preferred_element_type=jnp...  14.7 us
    dot_general x1, matrix products, per_device(): jnp.dot(pieces, lax.all_gather(out_weight, 'dp', axis=1, tiled=True), pre...  14.5 us
    dot_general x1, matrix products, per_device(): jnp.einsum('qhd,khd->hqk', request_vectors, address_vectors, preferred_el...  13.5 us
    reduce_sum x1, other arithmetic, per_device(): jnp.sum(near_w, axis=-1, keepdims=True)  11.2 us
    unnamed x5, local copies, waits for them, and re-layouts  10.3 us
  transfers between devices with their start and end apart: 3, of which 1 were waited for; matrix products, arithmetic and copies ran while one was open for 22% of the time, Pallas kernels for 0%

commit v1 on v0

v1 whole, which is shorter than its diff:
```python
import functools
import math

import jax
import jax.numpy as jnp
from jax import lax
from jax.experimental import pallas as pl
from jax.experimental.pallas import tpu as pltpu
from jax.sharding import PartitionSpec as P

CHANNEL_WIDTH = 128
SEGMENT_LENGTH = 256
MESH = pl.DeviceIdType.MESH
MEAN_ROWS = 8


def nearest_first(position, count):
    return sorted((e for e in range(count) if e != position), key=lambda e: (abs(e - position), e))


def fused(
    n, m, q_hbm, k_hbm, v_hbm, w_hbm, out_hbm,
    q_buf, k_buf, v_buf, w_buf, att, means, far_k, far_v, stage,
    load_sem, halo_send, halo_recv, mean_send, mean_recv,
    z_send, w_send, w_recv, out_sem,
):
    rows, feature = q_hbm.shape
    cols = w_hbm.shape[1]
    heads = feature // CHANNEL_WIDTH
    seg = SEGMENT_LENGTH
    local_blocks = rows // seg
    chunks = MEAN_ROWS // local_blocks
    chunk_width = feature // chunks
    chunk_heads = heads // chunks
    piece = feature // n
    p = lax.axis_index("seq")
    d = lax.axis_index("dp")

    barrier = pltpu.get_barrier_semaphore()

    def greet(i, carry):
        pl.semaphore_signal(barrier, inc=1, device_id=(lax.rem(p + i, n), d), device_id_type=MESH)
        return carry

    lax.fori_loop(1, n, greet, 0)

    @pl.when(d > 0)
    def _():
        pl.semaphore_signal(barrier, inc=1, device_id=(p, d - 1), device_id_type=MESH)

    @pl.when(d < m - 1)
    def _():
        pl.semaphore_signal(barrier, inc=1, device_id=(p, d + 1), device_id_type=MESH)

    load_k = pltpu.make_async_copy(k_hbm, k_buf.at[pl.ds(seg, rows)], load_sem.at[0])
    load_v = pltpu.make_async_copy(v_hbm, v_buf.at[pl.ds(seg, rows)], load_sem.at[1])
    load_q = pltpu.make_async_copy(q_hbm, q_buf, load_sem.at[2])
    load_w = pltpu.make_async_copy(w_hbm, w_buf.at[d], load_sem.at[3])
    for load in (load_k, load_v, load_q, load_w):
        load.start()

    @pl.when(p == 0)
    def _():
        k_buf[0:seg, :] = jnp.zeros((seg, feature), k_buf.dtype)
        v_buf[0:seg, :] = jnp.zeros((seg, feature), v_buf.dtype)

    far_k[...] = jnp.zeros_like(far_k)
    far_v[...] = jnp.zeros_like(far_v)

    z_count = jnp.where(d > 0, 1, 0) + jnp.where(d < m - 1, 1, 0)
    pl.semaphore_wait(barrier, n - 1 + z_count)

    last = pl.ds(rows - seg, seg)
    halo = [
        pltpu.make_async_remote_copy(
            src_ref=src.at[last], dst_ref=dst.at[pl.ds(0, seg)],
            send_sem=halo_send.at[i], recv_sem=halo_recv.at[i],
            device_id=(lax.rem(p + 1, n), d), device_id_type=MESH,
        )
        for i, (src, dst) in enumerate(((k_hbm, k_buf), (v_hbm, v_buf)))
    ]

    my_rows = pl.ds(pl.multiple_of(p * piece, piece), piece)

    def z_own(side, target):
        return pltpu.make_async_remote_copy(
            src_ref=w_hbm.at[my_rows], dst_ref=w_buf.at[d, my_rows],
            send_sem=z_send.at[side], recv_sem=w_recv.at[d, p],
            device_id=(p, target), device_id_type=MESH,
        )

    @pl.when(d > 0)
    def _():
        z_own(0, d - 1).start()

    @pl.when(d < m - 1)
    def _():
        z_own(1, d + 1).start()

    @pl.when(p < n - 1)
    def _():
        for copy in halo:
            copy.start()

    tables = [nearest_first(e, m) for e in range(m)]
    sources = []
    for j in range(m - 1):
        e = 0
        for at in range(m):
            e = e + jnp.where(d == at, tables[at][j], 0)
        sources.append(e)
    bits = []
    b = 2
    while b < n:
        bits.append(b)
        b *= 2
    core = lax.rem(p, 2)
    flips = [bit * (1 - 2 * lax.rem(p // bit, 2)) for bit in bits]
    hops = [flips[s] + core * (flips[-1 - s] - flips[s]) for s in range(len(bits))]
    hops.append(1 - 2 * core)
    stages = len(hops)

    def w_rows(r):
        return pl.ds(pl.multiple_of(r * piece, piece), piece)

    def w_copy(j, slot, r, target):
        ref = w_buf.at[sources[j], w_rows(r)]
        return pltpu.make_async_remote_copy(
            src_ref=ref, dst_ref=ref,
            send_sem=w_send.at[j, slot], recv_sem=w_recv.at[sources[j], r],
            device_id=target, device_id_type=MESH,
        )

    def arrivals(s):
        if s == 0:
            return [p]
        held = [p]
        for hop in hops[: s - 1]:
            held = held + [r + hop for r in held]
        return [r + hops[s - 1] for r in held]

    sent = []

    def serve(j, s):
        e = sources[j]
        for at, r in enumerate(arrivals(s)):
            w_copy(j, 0, r, (p, d)).wait_recv()
            if s == 0:
                onward = jnp.where(e < d, d + 1, d - 1)

                @pl.when(jnp.logical_and(onward >= 0, onward < m))
                def _():
                    pltpu.make_async_remote_copy(
                        src_ref=w_buf.at[e, my_rows], dst_ref=w_buf.at[e, my_rows],
                        send_sem=z_send.at[2 + j], recv_sem=w_recv.at[e, p],
                        device_id=(p, onward), device_id_type=MESH,
                    ).start()
            for later in range(s, stages):
                slot = len([1 for x in sent if x[0] == j])
                copy = w_copy(j, slot, r, (p + hops[later], d))
                copy.start()
                sent.append((j, copy))

    load_k.wait()
    load_v.wait()
    ones = jnp.ones((MEAN_ROWS, seg), jnp.bfloat16)
    row_index = lax.broadcasted_iota(jnp.int32, (MEAN_ROWS, chunk_width), 0)
    packed = []
    for buf in (k_buf, v_buf):
        part = jnp.zeros((MEAN_ROWS, chunk_width), jnp.float32)
        for i in range(local_blocks):
            for c in range(chunks):
                block = buf[seg * (i + 1) : seg * (i + 2), c * chunk_width : (c + 1) * chunk_width]
                total = jnp.dot(ones, block, preferred_element_type=jnp.float32)
                part = jnp.where(row_index == c * local_blocks + i, total * (1.0 / seg), part)
        packed.append(part)
    means[p] = jnp.concatenate(packed, axis=0).astype(means.dtype)

    def mean_copy(i, source):
        return pltpu.make_async_remote_copy(
            src_ref=means.at[source], dst_ref=means.at[source],
            send_sem=mean_send.at[i], recv_sem=mean_recv.at[source],
            device_id=(lax.rem(p + i, n), d), device_id_type=MESH,
        )

    def send_mean(i, carry):
        mean_copy(i, p).start()
        return carry

    lax.fori_loop(1, n - p, send_mean, 0)

    def unpack(at, carry):
        @pl.when(at < p)
        def _():
            mean_copy(1, at).wait_recv()

        both = means[at].astype(jnp.float32)
        to = pl.ds(pl.multiple_of(at * MEAN_ROWS, MEAN_ROWS), MEAN_ROWS)
        far_k[to, :] = both[:MEAN_ROWS]
        far_v[to, :] = both[MEAN_ROWS:]
        return carry

    load_q.wait()
    lax.fori_loop(0, p + 1, unpack, 0)

    scale = math.log2(math.e) / math.sqrt(CHANNEL_WIDTH)
    far_bias = math.log2(seg)
    contract = (((1,), (1,)), ((), ()))

    def head(i, h):
        lanes = pl.ds(pl.multiple_of(h * CHANNEL_WIDTH, CHANNEL_WIDTH), CHANNEL_WIDTH)
        q = q_buf[seg * i : seg * (i + 1), lanes]
        chunk = h // chunk_heads
        within = pl.ds(pl.multiple_of(lax.rem(h, chunk_heads) * CHANNEL_WIDTH, CHANNEL_WIDTH), CHANNEL_WIDTH)
        fk = far_k[:, within].astype(jnp.bfloat16)
        fv = far_v[:, within].astype(jnp.bfloat16)
        before = lax.dot_general(q, k_buf[seg * i : seg * (i + 1), lanes], contract, preferred_element_type=jnp.float32) * scale
        inside = lax.dot_general(q, k_buf[seg * (i + 1) : seg * (i + 2), lanes], contract, preferred_element_type=jnp.float32) * scale
        far = lax.dot_general(q, fk, contract, preferred_element_type=jnp.float32) * scale
        if i == 0:
            before = before + jnp.where(p == 0, -jnp.inf, 0.0)
        q_at = lax.broadcasted_iota(jnp.int32, (seg, seg), 0)
        k_at = lax.broadcasted_iota(jnp.int32, (seg, seg), 1)
        inside = jnp.where(k_at <= q_at, inside, -jnp.inf)
        slot = lax.broadcasted_iota(jnp.int32, (1, n * MEAN_ROWS), 1)
        in_tile = lax.rem(slot, MEAN_ROWS)
        block = (slot // MEAN_ROWS) * local_blocks + lax.rem(in_tile, local_blocks)
        usable = jnp.logical_and(in_tile // local_blocks == chunk, block < p * local_blocks + i - 1)
        far = far + jnp.where(usable, far_bias, -jnp.inf)
        top = jnp.maximum(
            jnp.max(jnp.maximum(before, inside), axis=1, keepdims=True),
            jnp.max(far, axis=1, keepdims=True),
        )
        before = jnp.exp2(before - top)
        inside = jnp.exp2(inside - top)
        far = jnp.exp2(far - top)
        total = jnp.sum(before + inside, axis=1, keepdims=True) + jnp.sum(far, axis=1, keepdims=True)
        mixed = jnp.dot(before.astype(jnp.bfloat16), v_buf[seg * i : seg * (i + 1), lanes], preferred_element_type=jnp.float32)
        mixed += jnp.dot(inside.astype(jnp.bfloat16), v_buf[seg * (i + 1) : seg * (i + 2), lanes], preferred_element_type=jnp.float32)
        mixed += jnp.dot(far.astype(jnp.bfloat16), fv, preferred_element_type=jnp.float32)
        att[seg * i : seg * (i + 1), lanes] = (mixed / total).astype(att.dtype)

    def attend(i):
        def pair(g, carry):
            head(i, 2 * g)
            head(i, 2 * g + 1)
            return carry

        lax.fori_loop(0, heads // 2, pair, 0)

    tile = min(256, cols)

    def out_copy(slot, e):
        to = pl.ds(pl.multiple_of(e * cols, cols), cols)
        return pltpu.make_async_copy(stage.at[slot], out_hbm.at[:, to], out_sem.at[slot])

    def project(count, e):
        slot = count % 2
        if count >= 2:
            out_copy(slot, e).wait()

        def one(t, carry):
            lanes = pl.ds(pl.multiple_of(t * tile, tile), tile)
            stage[slot, :, lanes] = jnp.dot(
                att[...], w_buf[e, :, lanes], preferred_element_type=jnp.float32
            ).astype(stage.dtype)
            return carry

        lax.fori_loop(0, cols // tile, one, 0)
        out_copy(slot, e).start()

    order = sorted(
        ((j, s) for j in range(m - 1) for s in range(stages + 1)), key=lambda js: (2 * js[0] + js[1], js[1])
    )
    due = list(order)

    def serve_next(count):
        for _ in range(min(count, len(due))):
            serve(*due.pop(0))

    for i in range(1, local_blocks):
        attend(i)
    serve_next(2)

    @pl.when(p > 0)
    def _():
        for copy in halo:
            copy.wait_recv()

    attend(0)
    load_w.wait()
    serve_next(2)
    project(0, d)
    done = 0
    while due:
        j, s = due[0]
        serve_next(1)
        if s == stages:
            done += 1
            project(done, sources[j])

    for count in range(max(0, m - 2), m):
        out_copy(count % 2, d).wait()

    @pl.when(d > 0)
    def _():
        z_own(0, d - 1).wait_send()

    @pl.when(d < m - 1)
    def _():
        z_own(1, d + 1).wait_send()

    for j in range(m - 1):
        e = sources[j]
        onward = jnp.where(e < d, d + 1, d - 1)

        @pl.when(jnp.logical_and(onward >= 0, onward < m))
        def _():
            pltpu.make_async_remote_copy(
                src_ref=w_buf.at[e, my_rows], dst_ref=w_buf.at[e, my_rows],
                send_sem=z_send.at[2 + j], recv_sem=w_recv.at[e, p],
                device_id=(p, onward), device_id_type=MESH,
            ).wait_send()

    for _, copy in sent:
        copy.wait_send()

    @pl.when(p < n - 1)
    def _():
        for copy in halo:
            copy.wait_send()

    def mean_sent(i, carry):
        mean_copy(i, p).wait_send()
        return carry

    lax.fori_loop(1, n - p, mean_sent, 0)


def per_device(n, m, queries, keys, values, out_weight):
    rows, feature = queries.shape[1:]
    cols = out_weight.shape[1]
    local_blocks = rows // SEGMENT_LENGTH
    chunk_width = feature * local_blocks // MEAN_ROWS
    bf16 = jnp.bfloat16
    out = pl.pallas_call(
        functools.partial(fused, n, m),
        out_shape=jax.ShapeDtypeStruct((rows, m * cols), bf16),
        in_specs=[pl.BlockSpec(memory_space=pl.ANY)] * 4,
        out_specs=pl.BlockSpec(memory_space=pl.ANY),
        scratch_shapes=[
            pltpu.VMEM((rows, feature), bf16),
            pltpu.VMEM((rows + SEGMENT_LENGTH, feature), bf16),
            pltpu.VMEM((rows + SEGMENT_LENGTH, feature), bf16),
            pltpu.VMEM((m, feature, cols), bf16),
            pltpu.VMEM((rows, feature), bf16),
            pltpu.VMEM((n, 2 * MEAN_ROWS, chunk_width), bf16),
            pltpu.VMEM((n * MEAN_ROWS, chunk_width), jnp.float32),
            pltpu.VMEM((n * MEAN_ROWS, chunk_width), jnp.float32),
            pltpu.VMEM((2, rows, cols), bf16),
            pltpu.SemaphoreType.DMA((4,)),
            pltpu.SemaphoreType.DMA((2,)),
            pltpu.SemaphoreType.DMA((2,)),
            pltpu.SemaphoreType.DMA((n,)),
            pltpu.SemaphoreType.DMA((n,)),
            pltpu.SemaphoreType.DMA((m + 1,)),
            pltpu.SemaphoreType.DMA((m - 1, n - 1)),
            pltpu.SemaphoreType.DMA((m, n)),
            pltpu.SemaphoreType.DMA((2,)),
        ],
        compiler_params=pltpu.CompilerParams(
            collective_id=0, has_side_effects=True, vmem_limit_bytes=56 * 1024 * 1024
        ),
    )(queries[0], keys[0], values[0], out_weight)
    return out[None]


def solution(mesh):
    return jax.shard_map(
        functools.partial(per_device, mesh.shape["seq"], mesh.shape["dp"]),
        mesh=mesh,
        in_specs=(P("dp", "seq", None), P("dp", "seq", None), P("dp", "seq", None), P(None, "dp")),
        out_specs=P("dp", "seq", None),
        check_vma=False,
    )
```

time: 320 us -> 122 us (0.38)
  waiting for transfers between devices: 192 us -> 0 us
  Pallas kernels: 0 us -> 117 us
  matrix products: 48 us -> 0 us
  blocking collectives: 23.6 us -> 0 us
  local copies, waits for them, and re-layouts: 20.7 us -> 4.7 us
  other arithmetic: 15.1 us -> 0 us
  between operations: 13.6 us -> 0.01 us
  starting transfers between devices: 5.58 us -> 0 us
    all_gather x1 -> x0, waiting for transfers between devices: 191 us -> none  [per_device(): lax.all_gather(out_weight, 'dp', axis=1, tiled=True)]
    pallas_call x0 -> x1, Pallas kernels: none -> 117 us  [per_device(): pl.pallas_call(functools.partial(fused, n, m), out_shape=jax.ShapeDtypeSt...]
    dot_general x5 -> x0, matrix products: 48 us -> none  [the longest x1 14.7 us: per_device(): jnp.einsum('hqk,khd->qhd', near_p, value_rows, preferred_element_type=jnp...]
    all_gather x2 -> x0, blocking collectives: 23.6 us -> none  [prefix(): pieces = jax.tree.map(lambda part: lax.all_gather(part, axis), value)]
    reduce_sum x4 -> x0, other arithmetic: 13.8 us -> none  [the longest x1 11.2 us: per_device(): jnp.sum(near_w, axis=-1, keepdims=True)]
    concatenate x2 -> x0, local copies, waits for them, and re-layouts: 5.62 us -> none  [per_device(): near_keys = jnp.concatenate([prev_keys, own_keys], axis=0)]
    unnamed x5 -> x1, local copies, waits for them, and re-layouts: 10.3 us -> 4.7 us
    ppermute x2 -> x0, starting transfers between devices: 5.58 us -> none  [shifted(): return lax.ppermute(block, axis, route)]
  transfers between devices with their start and end apart: 3 -> 0, of which waited for: 1 -> 0; matrix products, arithmetic and copies ran while one was open for 22% -> 0% of each run, Pallas kernels for 0% -> 0%
where the time goes in v1:
time: 122 us
  Pallas kernels  117 us (96%)
  local copies, waits for them, and re-layouts  4.7 us (4%)
    pallas_call x1, Pallas kernels, per_device(): pl.pallas_call(functools.partial(fused, n, m), out_shape=jax.ShapeDtypeSt...  117 us
    unnamed x1, local copies, waits for them, and re-layouts  4.7 us

profile of v1, /device:TPU:3, one launch (start us, length us, event | category | flops | bytes accessed | tf_op | source)
XLA Modules:
  0.0 121.6 jit_solution(15733194741436367951)
XLA Ops:
  0.0 116.9 %shard_map.46 = bf16[512,4096]{1,0:T(8,128)(2,1)} custom-call(bf16[512,2048]{1,0:T(8,128)(2,1)} %bitcast.5, bf16[512,2048]{1,0:T(8,128)(2,1)} %bitcast.6, bf16[512,2048]{1,0:T(8,128)(2,1)} %bitcast.7, bf16[2048,1024]{1,0:T(8,128)(2,1)} %w_hbm.1), custom_call_target="tpu_custom_call" | custom-call | tf_op jit(solution)/shard_map/pallas_call | solution.py:346
  116.9 4.7 %copy.6 = bf16[1,512,4096]{2,1,0:T(8,128)(2,1)} copy(bf16[1,512,4096]{2,1,0:T(8,128)(2,1)} %bitcast.4) | data formatting | bytes 8388608

commit v2 on v1

--- a/solution.py
+++ b/solution.py
@@ -11,6 +11,7 @@
 CHANNEL_WIDTH = 128
 SEGMENT_LENGTH = 256
 MESH = pl.DeviceIdType.MESH
+SUB = 1
 MEAN_ROWS = 8
 
 
@@ -32,7 +33,7 @@
     chunks = MEAN_ROWS // local_blocks
     chunk_width = feature // chunks
     chunk_heads = heads // chunks
-    piece = feature // n
+    piece = feature // (n * SUB)
     p = lax.axis_index("seq")
     d = lax.axis_index("dp")
 
@@ -70,37 +71,13 @@
     z_count = jnp.where(d > 0, 1, 0) + jnp.where(d < m - 1, 1, 0)
     pl.semaphore_wait(barrier, n - 1 + z_count)
 
-    last = pl.ds(rows - seg, seg)
-    halo = [
-        pltpu.make_async_remote_copy(
-            src_ref=src.at[last], dst_ref=dst.at[pl.ds(0, seg)],
+    def halo_copy(i):
+        src, dst = ((k_hbm, k_buf), (v_hbm, v_buf))[i]
+        return pltpu.make_async_remote_copy(
+            src_ref=src.at[pl.ds(rows - seg, seg)], dst_ref=dst.at[pl.ds(0, seg)],
             send_sem=halo_send.at[i], recv_sem=halo_recv.at[i],
             device_id=(lax.rem(p + 1, n), d), device_id_type=MESH,
         )
-        for i, (src, dst) in enumerate(((k_hbm, k_buf), (v_hbm, v_buf)))
-    ]
-
-    my_rows = pl.ds(pl.multiple_of(p * piece, piece), piece)
-
-    def z_own(side, target):
-        return pltpu.make_async_remote_copy(
-            src_ref=w_hbm.at[my_rows], dst_ref=w_buf.at[d, my_rows],
-            send_sem=z_send.at[side], recv_sem=w_recv.at[d, p],
-            device_id=(p, target), device_id_type=MESH,
-        )
-
-    @pl.when(d > 0)
-    def _():
-        z_own(0, d - 1).start()
-
-    @pl.when(d < m - 1)
-    def _():
-        z_own(1, d + 1).start()
-
-    @pl.when(p < n - 1)
-    def _():
-        for copy in halo:
-            copy.start()
 
     tables = [nearest_first(e, m) for e in range(m)]
     sources = []
@@ -109,57 +86,134 @@
         for at in range(m):
             e = e + jnp.where(d == at, tables[at][j], 0)
         sources.append(e)
+
     bits = []
     b = 2
     while b < n:
         bits.append(b)
         b *= 2
+    bits = bits[::-1]
     core = lax.rem(p, 2)
     flips = [bit * (1 - 2 * lax.rem(p // bit, 2)) for bit in bits]
-    hops = [flips[s] + core * (flips[-1 - s] - flips[s]) for s in range(len(bits))]
-    hops.append(1 - 2 * core)
-    stages = len(hops)
-
-    def w_rows(r):
-        return pl.ds(pl.multiple_of(r * piece, piece), piece)
-
-    def w_copy(j, slot, r, target):
-        ref = w_buf.at[sources[j], w_rows(r)]
+    peer = 1 - 2 * core
+
+    def plan(roots, hops):
+        held, events = [], []
+        for at, root in enumerate(roots):
+            held.append((p + root, 1 - 2 * at))
+            events.append((p + root, list(hops), True))
+        for s, hop in enumerate(hops):
+            new = [(r + sign * hop, sign) for r, sign in held]
+            events += [(r, list(hops[s + 1 :]), False) for r, _ in new]
+            held += new
+        return events
+
+    plans = (
+        plan([0], flips),
+        plan([0, sum(flips)], flips[:-1]) if bits else plan([0], flips),
+    )
+
+    def pick(even, odd):
+        return even + core * (odd - even)
+
+    events = []
+    for even, odd in zip(*plans):
+        targets = []
+        for at in range(max(len(even[1]), len(odd[1]))):
+            if at >= len(odd[1]):
+                targets.append((0, even[1][at]))
+            elif at >= len(even[1]):
+                targets.append((1, odd[1][at]))
+            else:
+                targets.append((None, pick(even[1][at], odd[1][at])))
+        targets.append((None, peer))
+        root = None if even[2] and odd[2] else 0 if even[2] else 1 if odd[2] else 2
+        events.append((pick(even[0], odd[0]), targets, root))
+    peer_pieces = [r + peer for r, _, _ in events]
+    roots = [(r, root) for r, _, root in events if root != 2]
+
+    def on_core(which, run):
+        if which is None:
+            run()
+        else:
+            pl.when(core == which)(run)
+
+    def w_rows(r, u):
+        return pl.ds(pl.multiple_of((r * SUB + u) * piece, piece), piece)
+
+    def z_own(at, u, side):
+        r = roots[at][0]
+        return pltpu.make_async_remote_copy(
+            src_ref=w_hbm.at[w_rows(r, u)], dst_ref=w_buf.at[d, w_rows(r, u)],
+            send_sem=z_send.at[side, at, u], recv_sem=w_recv.at[d, r, u],
+            device_id=(p, d - 1 + 2 * side), device_id_type=MESH,
+        )
+
+    def each_own(act):
+        for u in range(SUB):
+            for at, (_, root) in enumerate(roots):
+                for side in range(2):
+                    has = d > 0 if side == 0 else d < m - 1
+                    if root is not None:
+                        has = jnp.logical_and(has, core == root)
+
+                    @pl.when(has)
+                    def _():
+                        act(z_own(at, u, side))
+
+    each_own(lambda copy: copy.start())
+
+    @pl.when(p < n - 1)
+    def _():
+        halo_copy(0).start()
+        halo_copy(1).start()
+
+    def w_copy(j, u, slot, r, target):
+        ref = w_buf.at[sources[j], w_rows(r, u)]
         return pltpu.make_async_remote_copy(
             src_ref=ref, dst_ref=ref,
-            send_sem=w_send.at[j, slot], recv_sem=w_recv.at[sources[j], r],
+            send_sem=w_send.at[j, u, slot], recv_sem=w_recv.at[sources[j], r, u],
             device_id=target, device_id_type=MESH,
         )
 
-    def arrivals(s):
-        if s == 0:
-            return [p]
-        held = [p]
-        for hop in hops[: s - 1]:
-            held = held + [r + hop for r in held]
-        return [r + hops[s - 1] for r in held]
-
-    sent = []
-
-    def serve(j, s):
+    def z_onward(j, u, at, act):
+        r, root = roots[at]
         e = sources[j]
-        for at, r in enumerate(arrivals(s)):
-            w_copy(j, 0, r, (p, d)).wait_recv()
-            if s == 0:
-                onward = jnp.where(e < d, d + 1, d - 1)
-
-                @pl.when(jnp.logical_and(onward >= 0, onward < m))
-                def _():
-                    pltpu.make_async_remote_copy(
-                        src_ref=w_buf.at[e, my_rows], dst_ref=w_buf.at[e, my_rows],
-                        send_sem=z_send.at[2 + j], recv_sem=w_recv.at[e, p],
-                        device_id=(p, onward), device_id_type=MESH,
-                    ).start()
-            for later in range(s, stages):
-                slot = len([1 for x in sent if x[0] == j])
-                copy = w_copy(j, slot, r, (p + hops[later], d))
-                copy.start()
-                sent.append((j, copy))
+        onward = jnp.where(e < d, d + 1, d - 1)
+        has = jnp.logical_and(onward >= 0, onward < m)
+        if root is not None:
+            has = jnp.logical_and(has, core == root)
+
+        @pl.when(has)
+        def _():
+            act(pltpu.make_async_remote_copy(
+                src_ref=w_buf.at[e, w_rows(r, u)], dst_ref=w_buf.at[e, w_rows(r, u)],
+                send_sem=z_send.at[2 + j, at, u], recv_sem=w_recv.at[e, r, u],
+                device_id=(p, onward), device_id_type=MESH,
+            ))
+
+    def serve(j, u, i):
+        r, targets, root = events[i]
+        w_copy(j, u, 0, r, (p, d)).wait_recv()
+        if root != 2:
+            z_onward(j, u, i, lambda copy: copy.start())
+        for at, (which, target) in enumerate(targets):
+            on_core(which, w_copy(j, u, first_slot[i] + at, r, (p + target, d)).start)
+
+    first_slot = [sum(len(event[1]) for event in events[:i]) for i in range(len(events))]
+
+    def each_sent(act):
+        for j in range(m - 1):
+            for u in range(SUB):
+                for i, (r, targets, _) in enumerate(events):
+                    for at, (which, target) in enumerate(targets):
+                        copy = w_copy(j, u, first_slot[i] + at, r, (p + target, d))
+                        on_core(which, functools.partial(act, copy))
+
+    def finish(j):
+        for u in range(SUB):
+            for r in peer_pieces:
+                w_copy(j, u, 0, r, (p, d)).wait_recv()
 
     load_k.wait()
     load_v.wait()
@@ -240,13 +294,14 @@
         mixed += jnp.dot(far.astype(jnp.bfloat16), fv, preferred_element_type=jnp.float32)
         att[seg * i : seg * (i + 1), lanes] = (mixed / total).astype(att.dtype)
 
-    def attend(i):
+    def attend(i, part, parts):
         def pair(g, carry):
             head(i, 2 * g)
             head(i, 2 * g + 1)
             return carry
 
-        lax.fori_loop(0, heads // 2, pair, 0)
+        count = heads // 2 // parts
+        lax.fori_loop(part * count, (part + 1) * count, pair, 0)
 
     tile = min(256, cols)
 
@@ -269,66 +324,67 @@
         lax.fori_loop(0, cols // tile, one, 0)
         out_copy(slot, e).start()
 
-    order = sorted(
-        ((j, s) for j in range(m - 1) for s in range(stages + 1)), key=lambda js: (2 * js[0] + js[1], js[1])
-    )
-    due = list(order)
-
-    def serve_next(count):
-        for _ in range(min(count, len(due))):
-            serve(*due.pop(0))
-
-    for i in range(1, local_blocks):
-        attend(i)
-    serve_next(2)
-
-    @pl.when(p > 0)
-    def _():
-        for copy in halo:
-            copy.wait_recv()
-
-    attend(0)
-    load_w.wait()
-    serve_next(2)
-    project(0, d)
+    def halo_here():
+        @pl.when(p > 0)
+        def _():
+            halo_copy(0).wait_recv()
+            halo_copy(1).wait_recv()
+
+    def own_columns():
+        load_w.wait()
+        project(0, d)
+
+    parts = 4
+    early = [functools.partial(attend, i, part, parts) for i in range(1, local_blocks) for part in range(parts)]
+    late = [functools.partial(attend, 0, part, parts) for part in range(parts)]
+    half = len(early) // 2
+    for run in early[:half]:
+        run()
+    work = {0: early[half:], 2: [halo_here] + late[:2], 3: late[2:] + [own_columns]}
+
+    agenda = []
+    for j in range(m - 1):
+        for u in range(SUB):
+            for i, (_, _, root) in enumerate(events):
+                hops = bin(i).count("1")
+                if root == 1:
+                    agenda.append((j * SUB + u, j, u, i, 1))
+                    agenda.append((j * SUB + u + hops, j, u, i, 0))
+                else:
+                    agenda.append((j * SUB + u + hops, j, u, i, None))
+    agenda.sort(key=lambda entry: (entry[0], -entry[1], -entry[2], entry[3]))
+    deepest = max(entry[0] for entry in agenda) - ((m - 1) * SUB - 1)
+    levels = max((m - 1) * SUB + deepest, max(work) + 1)
     done = 0
-    while due:
-        j, s = due[0]
-        serve_next(1)
-        if s == stages:
+    for level in range(levels):
+        for due, j, u, i, which in agenda:
+            if due == level:
+                on_core(which, functools.partial(serve, j, u, i))
+        for run in work.get(level, []):
+            run()
+        while level >= max(work) and done < m - 1 and (done + 1) * SUB + deepest <= level:
+            finish(done)
             done += 1
-            project(done, sources[j])
+            project(done, sources[done - 1])
+    while done < m - 1:
+        finish(done)
+        done += 1
+        project(done, sources[done - 1])
 
     for count in range(max(0, m - 2), m):
         out_copy(count % 2, d).wait()
 
-    @pl.when(d > 0)
-    def _():
-        z_own(0, d - 1).wait_send()
-
-    @pl.when(d < m - 1)
-    def _():
-        z_own(1, d + 1).wait_send()
-
+    each_own(lambda copy: copy.wait_send())
     for j in range(m - 1):
-        e = sources[j]
-        onward = jnp.where(e < d, d + 1, d - 1)
-
-        @pl.when(jnp.logical_and(onward >= 0, onward < m))
-        def _():
-            pltpu.make_async_remote_copy(
-                src_ref=w_buf.at[e, my_rows], dst_ref=w_buf.at[e, my_rows],
-                send_sem=z_send.at[2 + j], recv_sem=w_recv.at[e, p],
-                device_id=(p, onward), device_id_type=MESH,
-            ).wait_send()
-
-    for _, copy in sent:
-        copy.wait_send()
+        for u in range(SUB):
+            for at in range(len(roots)):
+                z_onward(j, u, at, lambda copy: copy.wait_send())
+    each_sent(lambda copy: copy.wait_send())
 
     @pl.when(p < n - 1)
     def _():
-        for copy in halo:
-            copy.wait_send()
+        halo_copy(0).wait_send()
+        halo_copy(1).wait_send()
 
     def mean_sent(i, carry):
         mean_copy(i, p).wait_send()
@@ -363,9 +419,9 @@
             pltpu.SemaphoreType.DMA((2,)),
             pltpu.SemaphoreType.DMA((n,)),
             pltpu.SemaphoreType.DMA((n,)),
-            pltpu.SemaphoreType.DMA((m + 1,)),
-            pltpu.SemaphoreType.DMA((m - 1, n - 1)),
-            pltpu.SemaphoreType.DMA((m, n)),
+            pltpu.SemaphoreType.DMA((m + 1, 2, SUB)),
+            pltpu.SemaphoreType.DMA((m - 1, SUB, 2 * n)),
+            pltpu.SemaphoreType.DMA((m, n, SUB)),
             pltpu.SemaphoreType.DMA((2,)),
         ],
         compiler_params=pltpu.CompilerParams(

time: 122 us -> 112 us (0.918)
  Pallas kernels: 117 us -> 107 us
    pallas_call x1, Pallas kernels: 117 us -> 107 us  [per_device(): pl.pallas_call(functools.partial(fused, n, m), out_shape=jax.ShapeDtypeSt...]
where the time goes in v2:
time: 112 us
  Pallas kernels  107 us (96%)
  local copies, waits for them, and re-layouts  4.7 us (4%)
    pallas_call x1, Pallas kernels, per_device(): pl.pallas_call(functools.partial(fused, n, m), out_shape=jax.ShapeDtypeSt...  107 us
    unnamed x1, local copies, waits for them, and re-layouts  4.7 us

profile of v2, /device:TPU:3, one launch (start us, length us, event | category | flops | bytes accessed | tf_op | source)
XLA Modules:
  0.0 112.1 jit_solution(7323543038010810031)
XLA Ops:
  0.0 107.4 %shard_map.46 = bf16[512,4096]{1,0:T(8,128)(2,1)} custom-call(bf16[512,2048]{1,0:T(8,128)(2,1)} %bitcast.5, bf16[512,2048]{1,0:T(8,128)(2,1)} %bitcast.6, bf16[512,2048]{1,0:T(8,128)(2,1)} %bitcast.7, bf16[2048,1024]{1,0:T(8,128)(2,1)} %w_hbm.1), custom_call_target="tpu_custom_call" | custom-call | tf_op jit(solution)/shard_map/pallas_call | solution.py:402
  107.4 4.7 %copy.6 = bf16[1,512,4096]{2,1,0:T(8,128)(2,1)} copy(bf16[1,512,4096]{2,1,0:T(8,128)(2,1)} %bitcast.4) | data formatting | bytes 8388608
